TPU v7x, 1024 devices: a whole 4x8x16 slice. The times are simulated.
1024 devices in a mesh: seq: 64 (over z, y_lo, core), batch: 16 (over y_hi, x).
Axes of the slice: x: 4, y: 8 (y_hi: 4, y_lo: 2; y = y_hi * 2 + y_lo), z: 16, core: 2. Of those that a mesh axis runs over, the one named last changes fastest.
Arguments:
- inputs: bfloat16 [16, 64, 8192], P('batch'), may hold values from -6 to 6
- w_query: bfloat16 [8192, 8192], P('batch', 'seq'), may hold values from -0.0625 to 0.0625
- cache_keys: bfloat16 [16, 32768, 1024], P('batch', 'seq'), may hold values from -120 to 120
- cache_values: bfloat16 [16, 32768, 1024], P('batch', 'seq'), may hold values from -6 to 6
- lengths: int32 [16], P('batch'), may hold values from 1 to 32768, as said below
- positions: int32 [16, 64], P('batch'), may hold values from 0 to 32767, as said below
Outputs:
- attended: bfloat16 [16, 64, 8192], P('batch', None, 'seq')
Inputs may be any that keep to these rules, and one draw needn't show every extreme that they name: `lengths`: every sample has at least one valid position; some sample has all 32768 valid. `positions`: some query sits at position 0 and some at 32767.
All inputs are finite; a program needn't handle non-finite values.
Results may differ from a plain program's by a relative error of at most 0.015.
The roundings to bfloat16 on the way count: a program that leaves them out, or rounds other values in their place, can miss the bound.
Values may be sent and summed in bfloat16 or wider, within the bound.
A program may use at most 32 MiB of HBM per device.

v0:
```python
import jax
import jax.numpy as jnp
from jax import lax
from jax.sharding import PartitionSpec as P

H = 64
KVH = 8
HD = 128


def on_device(inputs, w_query, cache_keys, cache_values, lengths, positions):
    seq_count = lax.axis_size("seq")
    heads_here = H // seq_count
    group = H // KVH
    keys_here = cache_keys.shape[1]
    tokens = inputs[0]
    query_rows = tokens.shape[0]
    query = jnp.dot(
        tokens,
        lax.all_gather(w_query, "batch", axis=0, tiled=True),
        preferred_element_type=jnp.float32,
    )
    query = query.astype(jnp.bfloat16)
    all_query = lax.all_gather(query, "seq", axis=1, tiled=True)
    query_heads = all_query.reshape(query_rows, KVH, group, HD)
    key_pos = lax.axis_index("seq") * keys_here + jnp.arange(keys_here, dtype=jnp.int32)
    visible = (key_pos[None, :] <= positions[0][:, None]) & (key_pos[None, :] < lengths[0])
    key_rows = cache_keys[0]
    value_rows = cache_values[0]

    def one_head(kv_head):
        key_block = lax.dynamic_slice_in_dim(key_rows, kv_head * HD, HD, 1)
        value_block = lax.dynamic_slice_in_dim(value_rows, kv_head * HD, HD, 1)
        query_group = lax.dynamic_index_in_dim(query_heads, kv_head, 1, keepdims=False)
        score = jnp.einsum(
            "qrd,kd->rqk", query_group, key_block, preferred_element_type=jnp.float32
        ) * HD ** (-0.5)
        block_max = jnp.max(jnp.where(visible[None], score, -1e30), axis=-1)
        expo = jnp.where(visible[None], jnp.exp(score - block_max[..., None]), 0.0)
        block_total = jnp.sum(expo, axis=-1)
        prob = expo.astype(jnp.bfloat16)
        block_sum = jnp.einsum(
            "rqk,kd->rqd", prob, value_block, preferred_element_type=jnp.float32
        ).astype(jnp.bfloat16)
        return (block_sum, block_max, block_total)

    sums, maxima, totals = lax.map(one_head, jnp.arange(KVH, dtype=jnp.int32))
    sums = sums.reshape(1, H, query_rows, HD)
    maxima = maxima.reshape(1, H, query_rows)
    totals = totals.reshape(1, H, query_rows)
    got_sums = lax.all_to_all(sums, "seq", split_axis=1, concat_axis=0, tiled=True)
    got_max, got_total = (
        lax.all_to_all(maxima, "seq", split_axis=1, concat_axis=0, tiled=True),
        lax.all_to_all(totals, "seq", split_axis=1, concat_axis=0, tiled=True),
    )
    top = jnp.max(got_max, axis=0)
    weight = jnp.exp(got_max - top[None])
    numer = jnp.sum(weight[..., None] * got_sums.astype(jnp.float32), axis=0)
    denom = jnp.sum(weight * got_total, axis=0)
    result = numer / denom[..., None]
    return (
        jnp.transpose(result, (1, 0, 2))
        .reshape(query_rows, heads_here * HD)[None]
        .astype(jnp.bfloat16)
    )


def solution(mesh):
    in_specs = (
        P("batch", None, None),
        P("batch", "seq"),
        P("batch", "seq", None),
        P("batch", "seq", None),
        P("batch"),
        P("batch", None),
    )
    out_specs = P("batch", None, "seq")
    return jax.shard_map(
        on_device, mesh=mesh, in_specs=in_specs, out_specs=out_specs, check_vma=False
    )
```

profile of v0, /device:TPU:4, one launch (start us, length us, event | category | flops | bytes accessed | tf_op | source)
XLA Modules:
  0.0 381.6 jit_solution(2543762051252526885)
XLA Ops:
  7.3 87.0 %all-gather.3.cloned.1.call-done = bf16[8192,128]{1,0:T(8,128)(2,1)} async-done(((bf16[512,128]{1,0:T(8,128)(2,1)}), bf16[8192,128]{1,0:T(8,128)(2,1)}) %all-gather.3.cloned.1.call-update) | async-done | bytes 2097168 | tf_op jit(solution)/shard_map/all_gather | solution.py:20
  94.3 2.7 convolution_convert_fusion.1
  97.7 119.3 %all-gather.5.cloned.1.call-done = bf16[64,8192]{1,0:T(8,128)(2,1)} async-done(((bf16[64,128]{1,0:T(8,128)(2,1)}), bf16[64,8192]{1,0:T(8,128)(2,1)}) %all-gather.5.cloned.1.call-update) | async-done | bytes 1048592 | tf_op jit(solution)/shard_map/all_gather | solution.py:24
  217.0 1.5 copy.10
  218.5 55.3 %while.15 = (s32[]{:T(128)}, bf16[8,8,64,128]{3,2,1,0:T(8,128)(2,1)}, f32[8,8,64]{2,1,0:T(8,128)S(1)}, f32[8,8,64]{2,1,0:T(8,128)S(1)}, s32[8]{0:T(128)S(1)}, /*...) while((s32[]{:T(128)}, ...), condition=%wide.region_3.4_spmd.clone, body=%wide.region_0.3_spmd.clone.sunk | while | flops 136707072 | bytes 4091393 | solution.py:47
  221.9 1.3 select_reduce_fusion.2
  223.5 1.9 fusion.30
  228.8 1.3 select_reduce_fusion.2
  230.4 1.9 fusion.30
  235.7 1.3 select_reduce_fusion.2
  237.3 1.9 fusion.30
  244.3 1.9 fusion.30
  249.5 1.3 select_reduce_fusion.2
  251.2 1.9 fusion.30
  256.4 1.3 select_reduce_fusion.2
  258.1 1.9 fusion.30
  263.3 1.3 select_reduce_fusion.2
  265.0 1.9 fusion.30
  270.2 1.3 select_reduce_fusion.2
  271.9 1.9 fusion.30
  273.8 21.6 %all_to_all.36 = f32[1,64,64]{2,0,1:T(1,128)S(1)} all-to-all(f32[1,64,64]{2,0,1:T(1,128)S(1)} %bitcast.77), channel_id=1, replica_groups=mesh['seq'=64,'batch'=16] {'seq'}, dimensions={1} | all-to-all | bytes 32768 | tf_op jit(solution)/shard_map/all_to_all | solution.py:53
  295.4 17.1 %all_to_all.37 = f32[1,64,64]{2,0,1:T(1,128)S(1)} all-to-all(f32[1,64,64]{2,0,1:T(1,128)S(1)} %bitcast.78), channel_id=1, replica_groups=mesh['seq'=64,'batch'=16] {'seq'}, dimensions={1} | all-to-all | bytes 32768 | tf_op jit(solution)/shard_map/all_to_all | solution.py:54
  312.5 4.7 %all-to-all-start.1 = ((bf16[1,64,64,128]{3,2,0,1:T(8,128)(2,1)}), bf16[1,64,64,128]{3,2,0,1:T(8,128)(2,1)S(1)}, u32[]{:S(2)}, u32[]{:S(2)}) async-start(bf16[1,64,64,128]{3,2,0,1:T(8,128)(2,1)} %bitcast.7), calls=%async_computation.1 | async-start | bytes 2097152 | tf_op jit(solution)/shard_map/all_to_all | solution.py:51
  317.3 56.0 %all-to-all-done.1 = bf16[1,64,64,128]{3,2,0,1:T(8,128)(2,1)S(1)} async-done(((bf16[1,64,64,128]{3,2,0,1:T(8,128)(2,1)}), bf16[1,64,64,128]{3,2,0,1:T(8,128)(2,1)S(1)}, u32[]{:S(2)}, u32[]{:S(2)}) %all-to-all-start.1) | async-done | bytes 1048608 | tf_op jit(solution)/shard_map/all_to_all | solution.py:51
  (60 shorter events, 12.2 us)
Async XLA Ops:
  6.5 87.8 %copy-start = (bf16[1,64,8192]{2,1,0:T(8,128)(2,1)S(1)}, bf16[1,64,8192]{2,1,0:T(8,128)(2,1)}, u32[]{:S(2)}) copy-start(bf16[1,64,8192]{2,1,0:T(8,128)(2,1)} %param.8) | copy-start | bytes 3145732
  6.5 87.8 %all-gather.3.cloned.1.call-start = ((), (), s32[]{:S(2)}) async-start(), calls=%async_computation.3 | async-start | bytes 2228224 | tf_op jit(solution)/shard_map/all_gather | solution.py:20
  7.3 211.3 %copy-start.1 = (s32[1,64]{1,0:T(1,128)S(1)}, s32[1,64]{1,0:T(1,128)}, u32[]{:S(2)}) copy-start(s32[1,64]{1,0:T(1,128)} %param.13) | copy-start | bytes 772
  7.3 209.7 %all-gather.5.cloned.1.call-start = ((), (), s32[]{:S(2)}) async-start(), calls=%async_computation.4 | async-start | bytes 1064960 | tf_op jit(solution)/shard_map/all_gather | solution.py:24
  312.5 60.8 %all-to-all-start.1 = ((bf16[1,64,64,128]{3,2,0,1:T(8,128)(2,1)}), bf16[1,64,64,128]{3,2,0,1:T(8,128)(2,1)S(1)}, u32[]{:S(2)}, u32[]{:S(2)}) async-start(bf16[1,64,64,128]{3,2,0,1:T(8,128)(2,1)} %bitcast.7), calls=%async_computation.1 | async-start | bytes 2097152 | tf_op jit(solution)/shard_map/all_to_all | solution.py:51
Sparse Core Ops, SparseCore 0:
  11.5 82.7 all-gather.2
  97.1 119.8 all-gather.4
where the time goes:
time: 383 us; the launch traced here: 382 us
  waiting for transfers between devices  263 us (69%)
  blocking collectives  38.7 us (10%)
  matrix products  28.3 us (7%)
  loops' own time  21 us (5%)
  between operations  14.1 us (4%)
  local copies, waits for them, and re-layouts  6.57 us (2%)
  other arithmetic  5.09 us (1%)
  starting transfers between devices  4.69 us (1%)
    all_gather x1, waiting for transfers between devices, on_device(): all_query = lax.all_gather(query, 'seq', axis=1, tiled=True)  119 us
    all_gather x1, waiting for transfers between devices, on_device(): lax.all_gather(w_query, 'batch', axis=0, tiled=True)  87 us
    all_to_all x1, waiting for transfers between devices, on_device(): lax.all_to_all(sums, 'seq', split_axis=1, concat_axis=0, tiled=True)  56 us
    all_to_all x1, blocking collectives, on_device(): lax.all_to_all(maxima, 'seq', split_axis=1, concat_axis=0, tiled=True)  21.6 us
    another operation x1, loops' own time, on_device(): sums, maxima, totals = lax.map(one_head, jnp.arange(KVH, dtype=jnp.int32))  21 us
    all_to_all x1, blocking collectives, on_device(): lax.all_to_all(totals, 'seq', split_axis=1, concat_axis=0, tiled=True)  17.1 us
    dot_general x8, matrix products, one_head(): jnp.einsum('rqk,kd->rqd', prob, value_block, preferred_element_type=jnp.f...  15.3 us
    dot_general x8, matrix products, one_head(): jnp.einsum('qrd,kd->rqk', query_group, key_block, preferred_element_type=...  10.3 us
  transfers between devices with their start and end apart: 3, of which 3 were waited for; matrix products, arithmetic and copies ran while one was open for 0% of the time, Pallas kernels for 0%

commit v1 on v0

v1 whole, which is shorter than its diff:
```python
import functools
import jax
import jax.numpy as jnp
from jax import lax
from jax.experimental import pallas as pl
from jax.experimental.pallas import tpu as pltpu
from jax.sharding import PartitionSpec as P

MESH = pl.DeviceIdType.MESH
HD = 128
QUAD = 4
NX = 4
NYH = 4
NZ = 16
UNITS = 4
ROWS = 64
DEPTH = 512
KEYS = 512
PAY = ROWS + 16
SCALE = HD ** (-0.5) * 1.4426950408889634
NEG = -1e30


def arrived(ref, sem):
    pltpu.make_async_copy(ref, ref, sem).wait()


def kernel(
    x_ref, w_ref, k_ref, v_ref, len_ref, pos_ref, o_ref,
    wbuf, xbuf, part, pbuf, qown, qbuf, kbuf, vbuf, bias, sbuf, outb, inb, coef,
    w_send, w_recv, x_send, x_recv, kv_send, kv_recv, p_send, p_recv, q_send, q_recv, o_send, o_recv,
):
    s = lax.axis_index("seq")
    b = lax.axis_index("batch")
    z, quad = s // QUAD, s % QUAD
    yh, x = b // NX, b % NX
    unit_of_me = 2 * (z // 8) + z % 2
    handler = (z // 2) % QUAD

    def at_seq(t):
        return {"seq": t, "batch": b}

    def at_batch(t):
        return {"seq": s, "batch": t}

    def z_of_unit(u):
        return 2 * quad + 8 * (u // 2) + u % 2

    def piece(j, xt):
        return x_ref.at[0, :, pl.ds(pl.multiple_of((j * NX + xt) * DEPTH, DEPTH), DEPTH)]

    def k_cols(g):
        return k_ref.at[0, :, pl.ds(pl.multiple_of(g * HD, HD), HD)]

    def v_cols(g):
        return v_ref.at[0, :, pl.ds(pl.multiple_of(g * HD, HD), HD)]

    mine = pl.ds(pl.multiple_of(quad * KEYS, KEYS), KEYS)

    pltpu.make_async_copy(w_ref, wbuf.at[yh], w_recv.at[yh]).start()
    for j in range(NYH):
        pltpu.make_async_copy(piece(j, x), xbuf.at[j, pl.ds(x * ROWS, ROWS)], x_recv.at[x * NYH + j]).start()
    for a in range(2):
        g = quad + QUAD * a
        pltpu.make_async_copy(k_cols(g), kbuf.at[a, mine], kv_recv.at[quad * 4 + a]).start()
        pltpu.make_async_copy(v_cols(g), vbuf.at[a, mine], kv_recv.at[quad * 4 + 2 + a]).start()

    barrier = pltpu.get_barrier_semaphore()

    def greet(t):
        pl.semaphore_signal(barrier, inc=1, device_id=t, device_id_type=MESH)

    for d in range(1, NYH):
        greet(at_batch(lax.rem(yh + d, NYH) * NX + x))
    for d in range(1, NX):
        greet(at_batch(yh * NX + lax.rem(x + d, NX)))
    for d in range(1, QUAD):
        greet(at_seq(z * QUAD + lax.rem(quad + d, QUAD)))

    def greet_z(i, carry):
        t = i * QUAD + handler
        u = i // QUAD
        owner = z_of_unit(u) * QUAD + i % QUAD

        @pl.when(t != s)
        def _():
            greet(at_seq(t))

        @pl.when(owner != s)
        def _():
            greet(at_seq(owner))

        return carry

    lax.fori_loop(0, NZ, greet_z, 0)

    lane = lax.broadcasted_iota(jnp.int32, (1, 2 * ROWS), 1)
    pos = pos_ref[...]
    last = jnp.minimum(jnp.concatenate([pos, pos], axis=1) + 1, len_ref[0])

    def fill_bias(i, carry):
        row = lax.broadcasted_iota(jnp.int32, (128, 2 * ROWS), 0) + (z * QUAD * KEYS + i * 128)
        bias[pl.ds(pl.multiple_of(i * 128, 128), 128), :] = jnp.where(row < last, 0.0, NEG)
        return carry

    lax.fori_loop(0, QUAD * KEYS // 128, fill_bias, 0)

    self_handled = (handler == quad).astype(jnp.int32)
    pl.semaphore_wait(barrier, 2 * NZ + 9 - 2 * self_handled)

    copies = []
    for d in (2, 1, 3):
        t = lax.rem(yh + d, NYH)
        copies.append(pltpu.make_async_remote_copy(
            src_ref=w_ref, dst_ref=wbuf.at[yh], send_sem=w_send.at[d], recv_sem=w_recv.at[yh],
            device_id=at_batch(t * NX + x), device_id_type=MESH))
        copies[-1].start()
        t = lax.rem(x + d, NX)
        for j in range(NYH):
            copies.append(pltpu.make_async_remote_copy(
                src_ref=piece(j, t), dst_ref=xbuf.at[j, pl.ds(x * ROWS, ROWS)],
                send_sem=x_send.at[d * NYH + j], recv_sem=x_recv.at[x * NYH + j],
                device_id=at_batch(yh * NX + t), device_id_type=MESH))
            copies[-1].start()

    for a in range(2):
        for d in range(1, QUAD):
            h = lax.rem(quad + d, QUAD)
            g = h + QUAD * a
            for what, (cols, buf) in enumerate(((k_cols, kbuf), (v_cols, vbuf))):
                copies.append(pltpu.make_async_remote_copy(
                    src_ref=cols(g), dst_ref=buf.at[a, mine],
                    send_sem=kv_send.at[d * 4 + what * 2 + a], recv_sem=kv_recv.at[quad * 4 + what * 2 + a],
                    device_id=at_seq(z * QUAD + h), device_id_type=MESH))
                copies[-1].start()

    for d in range(NYH):
        j = lax.rem(yh + d, NYH)
        arrived(wbuf.at[j], w_recv.at[j])
        for t in range(NX):
            arrived(xbuf.at[j, pl.ds(t * ROWS, ROWS)], x_recv.at[t * NYH + j])
        term = jnp.dot(xbuf[j], wbuf[j], preferred_element_type=jnp.float32)
        if d == 0:
            part[...] = term
        else:
            part[...] += term
    for d in (2, 1, 3):
        t = lax.rem(x + d, NX)
        copies.append(pltpu.make_async_remote_copy(
            src_ref=part.at[pl.ds(t * ROWS, ROWS)], dst_ref=pbuf.at[x],
            send_sem=p_send.at[d], recv_sem=p_recv.at[x],
            device_id=at_batch(yh * NX + t), device_id_type=MESH))
        copies[-1].start()
    pltpu.make_async_copy(part.at[pl.ds(x * ROWS, ROWS)], pbuf.at[x], p_recv.at[x]).start()
    for t in range(NX):
        arrived(pbuf.at[t], p_recv.at[t])
    qown[...] = (pbuf[0] + pbuf[1] + pbuf[2] + pbuf[3]).astype(jnp.bfloat16)

    my_rows = pl.ds(pl.multiple_of(quad * ROWS, ROWS), ROWS)
    q_slot = unit_of_me * QUAD + quad

    def q_copy(i):
        t = lax.rem(z + NZ // 2 + i, NZ) * QUAD + handler
        return t, pltpu.make_async_remote_copy(
            src_ref=qown, dst_ref=qbuf.at[unit_of_me, my_rows], send_sem=q_send.at[i], recv_sem=q_recv.at[q_slot],
            device_id=at_seq(t), device_id_type=MESH)

    def send_q(i, carry):
        t, copy = q_copy(i)

        @pl.when(t != s)
        def _():
            copy.start()

        @pl.when(t == s)
        def _():
            pltpu.make_async_copy(qown, qbuf.at[unit_of_me, my_rows], q_recv.at[q_slot]).start()

        return carry

    lax.fori_loop(0, NZ, send_q, 0)

    def o_copy(u, r):
        t = z_of_unit(u) * QUAD + r
        return t, pltpu.make_async_remote_copy(
            src_ref=outb.at[u, r], dst_ref=inb.at[z], send_sem=o_send.at[u * QUAD + r], recv_sem=o_recv.at[z],
            device_id=at_seq(t), device_id_type=MESH)

    width = QUAD * ROWS

    def attend(u, carry):
        a = u // 2

        @pl.when(u % 2 == 0)
        def _():
            for src in range(QUAD):
                part_rows = pl.ds(src * KEYS, KEYS)
                arrived(kbuf.at[a, part_rows], kv_recv.at[src * 4 + a])
                arrived(vbuf.at[a, part_rows], kv_recv.at[src * 4 + 2 + a])

        for r in range(QUAD):
            arrived(qbuf.at[u, pl.ds(r * ROWS, ROWS)], q_recv.at[u * QUAD + r])
        query = qbuf[u]

        def scores(c, top):
            rows = pl.ds(pl.multiple_of(c * KEYS, KEYS), KEYS)
            raw = lax.dot_general(
                kbuf[a, rows, :], query, (((1,), (1,)), ((), ())), preferred_element_type=jnp.float32
            )
            add = bias[rows, :]
            val = raw * SCALE + jnp.concatenate([add, add], axis=1)
            sbuf[rows, :] = val
            return jnp.maximum(top, jnp.max(val.reshape(KEYS // 8, 8, width), axis=0))

        top = lax.fori_loop(0, QUAD, scores, jnp.full((8, width), -3e38, jnp.float32))
        top = jnp.max(top, axis=0, keepdims=True)

        def weigh(c, carry):
            total, acc = carry
            rows = pl.ds(pl.multiple_of(c * KEYS, KEYS), KEYS)
            expo = jnp.exp2(sbuf[rows, :] - top)
            total = total + jnp.sum(expo.reshape(KEYS // 8, 8, width), axis=0)
            acc = acc + lax.dot_general(
                vbuf[a, rows, :], expo.astype(jnp.bfloat16), (((0,), (0,)), ((), ())),
                preferred_element_type=jnp.float32,
            )
            return total, acc

        total, acc = lax.fori_loop(
            0, QUAD, weigh,
            (jnp.zeros((8, width), jnp.float32), jnp.zeros((HD, width), jnp.float32)),
        )
        total = jnp.sum(total, axis=0, keepdims=True)

        def three(val):
            hi = val.astype(jnp.bfloat16).astype(jnp.float32)
            mid = (val - hi).astype(jnp.bfloat16).astype(jnp.float32)
            return hi, mid, val - hi - mid

        sub = lax.broadcasted_iota(jnp.int32, (16, width), 0)
        stats = jnp.zeros((16, width), jnp.float32)
        for i, val in enumerate(three(top) + three(total)):
            stats = jnp.where(sub == i, val, stats)
        stats = stats.astype(jnp.bfloat16)
        for half in range(2):
            block = acc[:, half * 128:(half + 1) * 128].T.astype(jnp.bfloat16)
            for r in range(2):
                slot = outb.at[u, half * 2 + r]
                slot[pl.ds(0, ROWS), :] = block[r * ROWS:(r + 1) * ROWS]
                slot[pl.ds(ROWS, 16), :] = stats[:, half * 128:(half + 1) * 128]
        for r in range(QUAD):
            t, copy = o_copy(u, r)

            @pl.when(t != s)
            def _():
                copy.start()

            @pl.when(t == s)
            def _():
                pltpu.make_async_copy(outb.at[u, r], inb.at[z], o_recv.at[z]).start()

        return carry

    lax.fori_loop(0, UNITS, attend, 0)

    for i in range(NZ):
        arrived(inb.at[i], o_recv.at[i])
    maxima, totals = [], []
    for i in range(NZ):
        st = inb[i, pl.ds(ROWS, 16), :].astype(jnp.float32)
        maxima.append(st[0:1] + st[1:2] + st[2:3])
        totals.append(st[3:4] + st[4:5] + st[5:6])
    top = functools.reduce(jnp.maximum, maxima)
    weights = [jnp.exp2(m - top) for m in maxima]
    denom = functools.reduce(jnp.add, [w * t for w, t in zip(weights, totals)])
    inverse = 1.0 / denom
    sub = lax.broadcasted_iota(jnp.int32, (128, 128), 0)
    table = jnp.zeros((128, 128), jnp.float32)
    for i in range(NZ):
        table = jnp.where(sub == i, weights[i] * inverse, table)
    coef[...] = table.T
    mine_rows = pl.ds(pl.multiple_of((quad % 2) * ROWS, ROWS), ROWS)
    cols = coef[mine_rows, :]
    result = jnp.zeros((ROWS, HD), jnp.float32)
    for i in range(NZ):
        result = result + cols[:, i:i + 1] * inb[i, pl.ds(0, ROWS), :].astype(jnp.float32)
    o_ref[0] = result.astype(jnp.bfloat16)

    for copy in copies:
        copy.wait_send()

    def left(i, carry):
        t, copy = q_copy(i)

        @pl.when(t != s)
        def _():
            copy.wait_send()

        t2, copy2 = o_copy(i // QUAD, i % QUAD)

        @pl.when(t2 != s)
        def _():
            copy2.wait_send()

        return carry

    lax.fori_loop(0, NZ, left, 0)


def on_device(inputs, w_query, cache_keys, cache_values, lengths, positions):
    any_spec = pl.BlockSpec(memory_space=pl.ANY)
    bf, f32 = jnp.bfloat16, jnp.float32
    dma = pltpu.SemaphoreType.DMA
    return pl.pallas_call(
        kernel,
        out_shape=jax.ShapeDtypeStruct((1, ROWS, HD), bf),
        in_specs=[any_spec] * 4 + [pl.BlockSpec(memory_space=pltpu.SMEM), pl.BlockSpec(memory_space=pltpu.VMEM)],
        out_specs=pl.BlockSpec(memory_space=pltpu.VMEM),
        scratch_shapes=[
            pltpu.VMEM((NYH, DEPTH, HD), bf),
            pltpu.VMEM((NYH, NX * ROWS, DEPTH), bf),
            pltpu.VMEM((NX * ROWS, HD), f32),
            pltpu.VMEM((NX, ROWS, HD), f32),
            pltpu.VMEM((ROWS, HD), bf),
            pltpu.VMEM((UNITS, QUAD * ROWS, HD), bf),
            pltpu.VMEM((2, QUAD * KEYS, HD), bf),
            pltpu.VMEM((2, QUAD * KEYS, HD), bf),
            pltpu.VMEM((QUAD * KEYS, 2 * ROWS), f32),
            pltpu.VMEM((QUAD * KEYS, QUAD * ROWS), f32),
            pltpu.VMEM((UNITS, QUAD, PAY, HD), bf),
            pltpu.VMEM((NZ, PAY, HD), bf),
            pltpu.VMEM((128, 128), f32),
            dma((NYH,)), dma((NYH,)),
            dma((NX * NYH,)), dma((NX * NYH,)),
            dma((QUAD * 4,)), dma((QUAD * 4,)),
            dma((NX,)), dma((NX,)),
            dma((NZ,)), dma((NZ,)),
            dma((NZ,)), dma((NZ,)),
        ],
        compiler_params=pltpu.CompilerParams(
            collective_id=0, has_side_effects=True, vmem_limit_bytes=40 * 2**20
        ),
    )(inputs, w_query, cache_keys, cache_values, lengths, positions)


def solution(mesh):
    in_specs = (
        P("batch", None, None),
        P("batch", "seq"),
        P("batch", "seq", None),
        P("batch", "seq", None),
        P("batch"),
        P("batch", None),
    )
    return jax.shard_map(
        on_device, mesh=mesh, in_specs=in_specs, out_specs=P("batch", None, "seq"), check_vma=False
    )
```

time: 383 us -> 90.1 us (0.24)
  the two profiles are of different devices: /device:TPU:4 before, /device:TPU:9 now
where the time goes in v1:
time: 90.1 us; the launch traced here: 89.8 us
  Pallas kernels  84 us (93%)
  local copies, waits for them, and re-layouts  5.18 us (6%)
    pallas_call x1, Pallas kernels, on_device(): pl.pallas_call(kernel, out_shape=jax.ShapeDtypeStruct((1, ROWS, HD), bf),...  84 us
    unnamed x11, local copies, waits for them, and re-layouts  5.18 us

profile of v1, /device:TPU:9, one launch (start us, length us, event | category | flops | bytes accessed | tf_op | source)
XLA Modules:
  0.0 89.8 jit_solution(14446036422007598444)
XLA Ops:
  0.0 0.0 copy-start.4
  0.7 0.0 copy-done.4
  0.7 0.0 copy-start
  0.7 1.2 %copy-done = bf16[1,64,8192]{2,1,0:T(8,128)(2,1)S(1)} copy-done((bf16[1,64,8192]{2,1,0:T(8,128)(2,1)S(1)}, bf16[1,64,8192]{2,1,0:T(8,128)(2,1)}, u32[]{:S(2)}) %copy-start) | copy-done | bytes 1048600
  1.9 0.0 copy-start.1
  1.9 1.2 %copy-done.1 = bf16[1,512,1024]{2,1,0:T(8,128)(2,1)S(1)} copy-done((bf16[1,512,1024]{2,1,0:T(8,128)(2,1)S(1)}, bf16[1,512,1024]{2,1,0:T(8,128)(2,1)}, u32[]{:S(2)}) %copy-start.1) | copy-done | bytes 1048600
  3.1 0.0 copy-start.2
  3.1 1.2 %copy-done.2 = bf16[1,512,1024]{2,1,0:T(8,128)(2,1)S(1)} copy-done((bf16[1,512,1024]{2,1,0:T(8,128)(2,1)S(1)}, bf16[1,512,1024]{2,1,0:T(8,128)(2,1)}, u32[]{:S(2)}) %copy-start.2) | copy-done | bytes 1048600
  4.4 0.0 copy-start.3
  4.4 0.9 %copy-done.3 = bf16[512,128]{1,0:T(8,128)(2,1)S(1)} copy-done((bf16[512,128]{1,0:T(8,128)(2,1)S(1)}, bf16[512,128]{1,0:T(8,128)(2,1)}, u32[]{:S(2)}) %copy-start.3) | copy-done | bytes 131096
  5.3 84.0 %shard_map.64 = bf16[1,64,128]{2,1,0:T(8,128)(2,1)S(1)} custom-call(bf16[1,64,8192]{2,1,0:T(8,128)(2,1)S(1)} %copy-done, bf16[512,128]{1,0:T(8,128)(2,1)S(1)} %copy-done.3, bf16[1,512,1024]{2,1,0:T(8,128)(2,1)S(1)} %copy-done.1, bf16[1,512,1024]{2,1,0:T(8,128)(2,1)S(1)} %copy-done.2, s32[1]{0:T(128)S(6)} %copy.8.len_ref, s32[1,64]{1,0:T(1,128)S(1)} %copy-done.4), custom_call_target="tpu_custom_call" | custom-call | tf_op jit(solution)/shard_map/pallas_call | solution.py:314
  89.2 0.6 copy.9
Async XLA Ops:
  0.0 0.7 copy-start.4
  0.7 1.2 %copy-start = (bf16[1,64,8192]{2,1,0:T(8,128)(2,1)S(1)}, bf16[1,64,8192]{2,1,0:T(8,128)(2,1)}, u32[]{:S(2)}) copy-start(bf16[1,64,8192]{2,1,0:T(8,128)(2,1)} %x_ref.1) | copy-start | bytes 3145732
  1.9 1.2 %copy-start.1 = (bf16[1,512,1024]{2,1,0:T(8,128)(2,1)S(1)}, bf16[1,512,1024]{2,1,0:T(8,128)(2,1)}, u32[]{:S(2)}) copy-start(bf16[1,512,1024]{2,1,0:T(8,128)(2,1)} %k_ref.1) | copy-start | bytes 3145732
  3.1 1.2 %copy-start.2 = (bf16[1,512,1024]{2,1,0:T(8,128)(2,1)S(1)}, bf16[1,512,1024]{2,1,0:T(8,128)(2,1)}, u32[]{:S(2)}) copy-start(bf16[1,512,1024]{2,1,0:T(8,128)(2,1)} %v_ref.1) | copy-start | bytes 3145732
  4.4 0.9 %copy-start.3 = (bf16[512,128]{1,0:T(8,128)(2,1)S(1)}, bf16[512,128]{1,0:T(8,128)(2,1)}, u32[]{:S(2)}) copy-start(bf16[512,128]{1,0:T(8,128)(2,1)} %w_ref.1) | copy-start | bytes 393220

commit v2 on v1

--- a/solution.py
+++ b/solution.py
@@ -29,6 +29,7 @@
     x_ref, w_ref, k_ref, v_ref, len_ref, pos_ref, o_ref,
     wbuf, xbuf, part, pbuf, qown, qbuf, kbuf, vbuf, bias, sbuf, outb, inb, coef,
     w_send, w_recv, x_send, x_recv, kv_send, kv_recv, p_send, p_recv, q_send, q_recv, o_send, o_recv,
+    plane_sem, group_sem,
 ):
     s = lax.axis_index("seq")
     b = lax.axis_index("batch")
@@ -70,25 +71,23 @@
     def greet(t):
         pl.semaphore_signal(barrier, inc=1, device_id=t, device_id_type=MESH)
 
+    watch = QUAD - 1
+    stand_in = jnp.where(quad == watch, s - 1, s)
     for d in range(1, NYH):
-        greet(at_batch(lax.rem(yh + d, NYH) * NX + x))
+        greet({"seq": stand_in, "batch": lax.rem(yh + d, NYH) * NX + x})
     for d in range(1, NX):
-        greet(at_batch(yh * NX + lax.rem(x + d, NX)))
-    for d in range(1, QUAD):
-        greet(at_seq(z * QUAD + lax.rem(quad + d, QUAD)))
+        greet({"seq": stand_in, "batch": yh * NX + lax.rem(x + d, NX)})
+    for q in range(QUAD - 1):
+        @pl.when(q != quad)
+        def _():
+            greet(at_seq(z * QUAD + q))
 
     def greet_z(i, carry):
-        t = i * QUAD + handler
-        u = i // QUAD
-        owner = z_of_unit(u) * QUAD + i % QUAD
+        t = lax.rem(z + i, NZ) * QUAD + watch
 
         @pl.when(t != s)
         def _():
             greet(at_seq(t))
-
-        @pl.when(owner != s)
-        def _():
-            greet(at_seq(owner))
 
         return carry
 
@@ -105,8 +104,18 @@
 
     lax.fori_loop(0, QUAD * KEYS // 128, fill_bias, 0)
 
-    self_handled = (handler == quad).astype(jnp.int32)
-    pl.semaphore_wait(barrier, 2 * NZ + 9 - 2 * self_handled)
+    @pl.when(quad < watch - 1)
+    def _():
+        pl.semaphore_wait(barrier, 9)
+
+    @pl.when(quad == watch - 1)
+    def _():
+        pl.semaphore_wait(barrier, 15)
+        pl.semaphore_signal(plane_sem, inc=1, device_id=at_seq(s + 1), device_id_type=MESH)
+
+    @pl.when(quad == watch)
+    def _():
+        pl.semaphore_wait(plane_sem, 1)
 
     copies = []
     for d in (2, 1, 3):
@@ -152,9 +161,20 @@
             device_id=at_batch(yh * NX + t), device_id_type=MESH))
         copies[-1].start()
     pltpu.make_async_copy(part.at[pl.ds(x * ROWS, ROWS)], pbuf.at[x], p_recv.at[x]).start()
+
+    @pl.when(quad == watch)
+    def _():
+        pl.semaphore_wait(barrier, NZ * QUAD - 1)
+        for d in range(1, QUAD):
+            pl.semaphore_signal(group_sem, inc=1, device_id=at_seq(s - d), device_id_type=MESH)
+
     for t in range(NX):
         arrived(pbuf.at[t], p_recv.at[t])
     qown[...] = (pbuf[0] + pbuf[1] + pbuf[2] + pbuf[3]).astype(jnp.bfloat16)
+
+    @pl.when(quad != watch)
+    def _():
+        pl.semaphore_wait(group_sem, 1)
 
     my_rows = pl.ds(pl.multiple_of(quad * ROWS, ROWS), ROWS)
     q_slot = unit_of_me * QUAD + quad
@@ -336,6 +356,7 @@
             dma((NX,)), dma((NX,)),
             dma((NZ,)), dma((NZ,)),
             dma((NZ,)), dma((NZ,)),
+            pltpu.SemaphoreType.REGULAR, pltpu.SemaphoreType.REGULAR,
         ],
         compiler_params=pltpu.CompilerParams(
             collective_id=0, has_side_effects=True, vmem_limit_bytes=40 * 2**20

time: 90.1 us -> 80.3 us (0.89)
  the two profiles are of different devices: /device:TPU:9 before, /device:TPU:75 now
where the time goes in v2:
time: 80.3 us; the launch traced here: 80 us
  Pallas kernels  74.1 us (92%)
  local copies, waits for them, and re-layouts  5.18 us (6%)
    pallas_call x1, Pallas kernels, on_device(): pl.pallas_call(kernel, out_shape=jax.ShapeDtypeStruct((1, ROWS, HD), bf),...  74.1 us
    unnamed x11, local copies, waits for them, and re-layouts  5.18 us

profile of v2, /device:TPU:75, one launch (start us, length us, event | category | flops | bytes accessed | tf_op | source)
XLA Modules:
  0.0 80.0 jit_solution(16050410983165492642)
XLA Ops:
  0.0 0.0 copy-start.4
  0.7 0.0 copy-done.4
  0.7 0.0 copy-start
  0.7 1.2 %copy-done = bf16[1,64,8192]{2,1,0:T(8,128)(2,1)S(1)} copy-done((bf16[1,64,8192]{2,1,0:T(8,128)(2,1)S(1)}, bf16[1,64,8192]{2,1,0:T(8,128)(2,1)}, u32[]{:S(2)}) %copy-start) | copy-done | bytes 1048600
  1.9 0.0 copy-start.1
  1.9 1.2 %copy-done.1 = bf16[1,512,1024]{2,1,0:T(8,128)(2,1)S(1)} copy-done((bf16[1,512,1024]{2,1,0:T(8,128)(2,1)S(1)}, bf16[1,512,1024]{2,1,0:T(8,128)(2,1)}, u32[]{:S(2)}) %copy-start.1) | copy-done | bytes 1048600
  3.1 0.0 copy-start.2
  3.1 1.2 %copy-done.2 = bf16[1,512,1024]{2,1,0:T(8,128)(2,1)S(1)} copy-done((bf16[1,512,1024]{2,1,0:T(8,128)(2,1)S(1)}, bf16[1,512,1024]{2,1,0:T(8,128)(2,1)}, u32[]{:S(2)}) %copy-start.2) | copy-done | bytes 1048600
  4.4 0.0 copy-start.3
  4.4 0.9 %copy-done.3 = bf16[512,128]{1,0:T(8,128)(2,1)S(1)} copy-done((bf16[512,128]{1,0:T(8,128)(2,1)S(1)}, bf16[512,128]{1,0:T(8,128)(2,1)}, u32[]{:S(2)}) %copy-start.3) | copy-done | bytes 131096
  5.3 74.1 %shard_map.64 = bf16[1,64,128]{2,1,0:T(8,128)(2,1)S(1)} custom-call(bf16[1,64,8192]{2,1,0:T(8,128)(2,1)S(1)} %copy-done, bf16[512,128]{1,0:T(8,128)(2,1)S(1)} %copy-done.3, bf16[1,512,1024]{2,1,0:T(8,128)(2,1)S(1)} %copy-done.1, bf16[1,512,1024]{2,1,0:T(8,128)(2,1)S(1)} %copy-done.2, s32[1]{0:T(128)S(6)} %copy.8.len_ref, s32[1,64]{1,0:T(1,128)S(1)} %copy-done.4), custom_call_target="tpu_custom_call" | custom-call | tf_op jit(solution)/shard_map/pallas_call | solution.py:334
  79.4 0.6 copy.9
Async XLA Ops:
  0.0 0.7 copy-start.4
  0.7 1.2 %copy-start = (bf16[1,64,8192]{2,1,0:T(8,128)(2,1)S(1)}, bf16[1,64,8192]{2,1,0:T(8,128)(2,1)}, u32[]{:S(2)}) copy-start(bf16[1,64,8192]{2,1,0:T(8,128)(2,1)} %x_ref.1) | copy-start | bytes 3145732
  1.9 1.2 %copy-start.1 = (bf16[1,512,1024]{2,1,0:T(8,128)(2,1)S(1)}, bf16[1,512,1024]{2,1,0:T(8,128)(2,1)}, u32[]{:S(2)}) copy-start(bf16[1,512,1024]{2,1,0:T(8,128)(2,1)} %k_ref.1) | copy-start | bytes 3145732
  3.1 1.2 %copy-start.2 = (bf16[1,512,1024]{2,1,0:T(8,128)(2,1)S(1)}, bf16[1,512,1024]{2,1,0:T(8,128)(2,1)}, u32[]{:S(2)}) copy-start(bf16[1,512,1024]{2,1,0:T(8,128)(2,1)} %v_ref.1) | copy-start | bytes 3145732
  4.4 0.9 %copy-start.3 = (bf16[512,128]{1,0:T(8,128)(2,1)S(1)}, bf16[512,128]{1,0:T(8,128)(2,1)}, u32[]{:S(2)}) copy-start(bf16[512,128]{1,0:T(8,128)(2,1)} %w_ref.1) | copy-start | bytes 393220

commit v3 on v2

--- a/solution.py
+++ b/solution.py
@@ -16,7 +16,6 @@
 ROWS = 64
 DEPTH = 512
 KEYS = 512
-PAY = ROWS + 16
 SCALE = HD ** (-0.5) * 1.4426950408889634
 NEG = -1e30
 
@@ -27,8 +26,8 @@
 
 def kernel(
     x_ref, w_ref, k_ref, v_ref, len_ref, pos_ref, o_ref,
-    wbuf, xbuf, part, pbuf, qown, qbuf, kbuf, vbuf, bias, sbuf, outb, inb, coef,
-    w_send, w_recv, x_send, x_recv, kv_send, kv_recv, p_send, p_recv, q_send, q_recv, o_send, o_recv,
+    wbuf, xbuf, part, pbuf, qown, qbuf, kbuf, vbuf, bias, sbuf, outb, inb, outs, ins, coef,
+    w_send, w_recv, x_send, x_recv, kv_send, kv_recv, p_send, p_recv, q_send, q_recv, o_send, o_recv, t_send, t_recv,
     plane_sem, group_sem,
 ):
     s = lax.axis_index("seq")
@@ -92,17 +91,6 @@
         return carry
 
     lax.fori_loop(0, NZ, greet_z, 0)
-
-    lane = lax.broadcasted_iota(jnp.int32, (1, 2 * ROWS), 1)
-    pos = pos_ref[...]
-    last = jnp.minimum(jnp.concatenate([pos, pos], axis=1) + 1, len_ref[0])
-
-    def fill_bias(i, carry):
-        row = lax.broadcasted_iota(jnp.int32, (128, 2 * ROWS), 0) + (z * QUAD * KEYS + i * 128)
-        bias[pl.ds(pl.multiple_of(i * 128, 128), 128), :] = jnp.where(row < last, 0.0, NEG)
-        return carry
-
-    lax.fori_loop(0, QUAD * KEYS // 128, fill_bias, 0)
 
     @pl.when(quad < watch - 1)
     def _():
@@ -142,6 +130,16 @@
                     send_sem=kv_send.at[d * 4 + what * 2 + a], recv_sem=kv_recv.at[quad * 4 + what * 2 + a],
                     device_id=at_seq(z * QUAD + h), device_id_type=MESH))
                 copies[-1].start()
+
+    pos = pos_ref[...]
+    last = jnp.minimum(jnp.concatenate([pos, pos], axis=1) + 1, len_ref[0])
+
+    def fill_bias(i, carry):
+        row = lax.broadcasted_iota(jnp.int32, (128, 2 * ROWS), 0) + (z * QUAD * KEYS + i * 128)
+        bias[pl.ds(pl.multiple_of(i * 128, 128), 128), :] = jnp.where(row < last, 0.0, NEG)
+        return carry
+
+    lax.fori_loop(0, QUAD * KEYS // 128, fill_bias, 0)
 
     for d in range(NYH):
         j = lax.rem(yh + d, NYH)
@@ -180,7 +178,8 @@
     q_slot = unit_of_me * QUAD + quad
 
     def q_copy(i):
-        t = lax.rem(z + NZ // 2 + i, NZ) * QUAD + handler
+        far = NZ + jnp.where(i % 2 == 1, (i + 1) // 2, -(i // 2))
+        t = lax.rem(z + far, NZ) * QUAD + handler
         return t, pltpu.make_async_remote_copy(
             src_ref=qown, dst_ref=qbuf.at[unit_of_me, my_rows], send_sem=q_send.at[i], recv_sem=q_recv.at[q_slot],
             device_id=at_seq(t), device_id_type=MESH)
@@ -202,9 +201,12 @@
 
     def o_copy(u, r):
         t = z_of_unit(u) * QUAD + r
-        return t, pltpu.make_async_remote_copy(
-            src_ref=outb.at[u, r], dst_ref=inb.at[z], send_sem=o_send.at[u * QUAD + r], recv_sem=o_recv.at[z],
-            device_id=at_seq(t), device_id_type=MESH)
+        return t, [
+            pltpu.make_async_remote_copy(
+                src_ref=src.at[u, r], dst_ref=dst.at[z], send_sem=send.at[u * QUAD + r], recv_sem=recv.at[z],
+                device_id=at_seq(t), device_id_type=MESH)
+            for src, dst, send, recv in ((outs, ins, t_send, t_recv), (outb, inb, o_send, o_recv))
+        ]
 
     width = QUAD * ROWS
 
@@ -232,7 +234,7 @@
             sbuf[rows, :] = val
             return jnp.maximum(top, jnp.max(val.reshape(KEYS // 8, 8, width), axis=0))
 
-        top = lax.fori_loop(0, QUAD, scores, jnp.full((8, width), -3e38, jnp.float32))
+        top = lax.fori_loop(0, QUAD, scores, jnp.full((8, width), -3e38, jnp.float32), unroll=True)
         top = jnp.max(top, axis=0, keepdims=True)
 
         def weigh(c, carry):
@@ -248,48 +250,38 @@
 
         total, acc = lax.fori_loop(
             0, QUAD, weigh,
-            (jnp.zeros((8, width), jnp.float32), jnp.zeros((HD, width), jnp.float32)),
+            (jnp.zeros((8, width), jnp.float32), jnp.zeros((HD, width), jnp.float32)), unroll=True,
         )
         total = jnp.sum(total, axis=0, keepdims=True)
 
-        def three(val):
-            hi = val.astype(jnp.bfloat16).astype(jnp.float32)
-            mid = (val - hi).astype(jnp.bfloat16).astype(jnp.float32)
-            return hi, mid, val - hi - mid
-
-        sub = lax.broadcasted_iota(jnp.int32, (16, width), 0)
-        stats = jnp.zeros((16, width), jnp.float32)
-        for i, val in enumerate(three(top) + three(total)):
-            stats = jnp.where(sub == i, val, stats)
-        stats = stats.astype(jnp.bfloat16)
         for half in range(2):
             block = acc[:, half * 128:(half + 1) * 128].T.astype(jnp.bfloat16)
             for r in range(2):
-                slot = outb.at[u, half * 2 + r]
-                slot[pl.ds(0, ROWS), :] = block[r * ROWS:(r + 1) * ROWS]
-                slot[pl.ds(ROWS, 16), :] = stats[:, half * 128:(half + 1) * 128]
+                outb[u, half * 2 + r] = block[r * ROWS:(r + 1) * ROWS]
+                outs[u, half * 2 + r, 0:1, :] = top[:, half * 128:(half + 1) * 128]
+                outs[u, half * 2 + r, 1:2, :] = total[:, half * 128:(half + 1) * 128]
         for r in range(QUAD):
-            t, copy = o_copy(u, r)
+            t, pair = o_copy(u, r)
 
             @pl.when(t != s)
             def _():
-                copy.start()
+                for copy in pair:
+                    copy.start()
 
             @pl.when(t == s)
             def _():
                 pltpu.make_async_copy(outb.at[u, r], inb.at[z], o_recv.at[z]).start()
+                pltpu.make_async_copy(outs.at[u, r], ins.at[z], t_recv.at[z]).start()
 
         return carry
 
     lax.fori_loop(0, UNITS, attend, 0)
 
-    for i in range(NZ):
-        arrived(inb.at[i], o_recv.at[i])
     maxima, totals = [], []
     for i in range(NZ):
-        st = inb[i, pl.ds(ROWS, 16), :].astype(jnp.float32)
-        maxima.append(st[0:1] + st[1:2] + st[2:3])
-        totals.append(st[3:4] + st[4:5] + st[5:6])
+        arrived(ins.at[i], t_recv.at[i])
+        maxima.append(ins[i, 0:1, :])
+        totals.append(ins[i, 1:2, :])
     top = functools.reduce(jnp.maximum, maxima)
     weights = [jnp.exp2(m - top) for m in maxima]
     denom = functools.reduce(jnp.add, [w * t for w, t in zip(weights, totals)])
@@ -303,7 +295,8 @@
     cols = coef[mine_rows, :]
     result = jnp.zeros((ROWS, HD), jnp.float32)
     for i in range(NZ):
-        result = result + cols[:, i:i + 1] * inb[i, pl.ds(0, ROWS), :].astype(jnp.float32)
+        arrived(inb.at[i], o_recv.at[i])
+        result = result + cols[:, i:i + 1] * inb[i].astype(jnp.float32)
     o_ref[0] = result.astype(jnp.bfloat16)
 
     for copy in copies:
@@ -320,7 +313,8 @@
 
         @pl.when(t2 != s)
         def _():
-            copy2.wait_send()
+            for one in copy2:
+                one.wait_send()
 
         return carry
 
@@ -347,13 +341,16 @@
             pltpu.VMEM((2, QUAD * KEYS, HD), bf),
             pltpu.VMEM((QUAD * KEYS, 2 * ROWS), f32),
             pltpu.VMEM((QUAD * KEYS, QUAD * ROWS), f32),
-            pltpu.VMEM((UNITS, QUAD, PAY, HD), bf),
-            pltpu.VMEM((NZ, PAY, HD), bf),
+            pltpu.VMEM((UNITS, QUAD, ROWS, HD), bf),
+            pltpu.VMEM((NZ, ROWS, HD), bf),
+            pltpu.VMEM((UNITS, QUAD, 2, 128), f32),
+            pltpu.VMEM((NZ, 2, 128), f32),
             pltpu.VMEM((128, 128), f32),
             dma((NYH,)), dma((NYH,)),
             dma((NX * NYH,)), dma((NX * NYH,)),
             dma((QUAD * 4,)), dma((QUAD * 4,)),
             dma((NX,)), dma((NX,)),
+            dma((NZ,)), dma((NZ,)),
             dma((NZ,)), dma((NZ,)),
             dma((NZ,)), dma((NZ,)),
             pltpu.SemaphoreType.REGULAR, pltpu.SemaphoreType.REGULAR,

time: 80.3 us -> 78.8 us (0.981)
  Pallas kernels: 74.1 us -> 72.6 us
    pallas_call x1, Pallas kernels: 74.1 us -> 72.6 us  [on_device(): pl.pallas_call(kernel, out_shape=jax.ShapeDtypeStruct((1, ROWS, HD), bf),...]
where the time goes in v3:
time: 78.8 us; the launch traced here: 78.5 us
  Pallas kernels  72.6 us (92%)
  local copies, waits for them, and re-layouts  5.18 us (7%)
    pallas_call x1, Pallas kernels, on_device(): pl.pallas_call(kernel, out_shape=jax.ShapeDtypeStruct((1, ROWS, HD), bf),...  72.6 us
    unnamed x11, local copies, waits for them, and re-layouts  5.18 us

profile of v3, /device:TPU:75, one launch (start us, length us, event | category | flops | bytes accessed | tf_op | source)
XLA Modules:
  0.0 78.5 jit_solution(8287083797692386223)
XLA Ops:
  0.0 0.0 copy-start.4
  0.7 0.0 copy-done.4
  0.7 0.0 copy-start
  0.7 1.2 %copy-done = bf16[1,64,8192]{2,1,0:T(8,128)(2,1)S(1)} copy-done((bf16[1,64,8192]{2,1,0:T(8,128)(2,1)S(1)}, bf16[1,64,8192]{2,1,0:T(8,128)(2,1)}, u32[]{:S(2)}) %copy-start) | copy-done | bytes 1048600
  1.9 0.0 copy-start.1
  1.9 1.2 %copy-done.1 = bf16[1,512,1024]{2,1,0:T(8,128)(2,1)S(1)} copy-done((bf16[1,512,1024]{2,1,0:T(8,128)(2,1)S(1)}, bf16[1,512,1024]{2,1,0:T(8,128)(2,1)}, u32[]{:S(2)}) %copy-start.1) | copy-done | bytes 1048600
  3.1 0.0 copy-start.2
  3.1 1.2 %copy-done.2 = bf16[1,512,1024]{2,1,0:T(8,128)(2,1)S(1)} copy-done((bf16[1,512,1024]{2,1,0:T(8,128)(2,1)S(1)}, bf16[1,512,1024]{2,1,0:T(8,128)(2,1)}, u32[]{:S(2)}) %copy-start.2) | copy-done | bytes 1048600
  4.4 0.0 copy-start.3
  4.4 0.9 %copy-done.3 = bf16[512,128]{1,0:T(8,128)(2,1)S(1)} copy-done((bf16[512,128]{1,0:T(8,128)(2,1)S(1)}, bf16[512,128]{1,0:T(8,128)(2,1)}, u32[]{:S(2)}) %copy-start.3) | copy-done | bytes 131096
  5.3 72.6 %shard_map.64 = bf16[1,64,128]{2,1,0:T(8,128)(2,1)S(1)} custom-call(bf16[1,64,8192]{2,1,0:T(8,128)(2,1)S(1)} %copy-done, bf16[512,128]{1,0:T(8,128)(2,1)S(1)} %copy-done.3, bf16[1,512,1024]{2,1,0:T(8,128)(2,1)S(1)} %copy-done.1, bf16[1,512,1024]{2,1,0:T(8,128)(2,1)S(1)} %copy-done.2, s32[1]{0:T(128)S(6)} %copy.8.len_ref, s32[1,64]{1,0:T(1,128)S(1)} %copy-done.4), custom_call_target="tpu_custom_call" | custom-call | tf_op jit(solution)/shard_map/pallas_call | solution.py:328
  77.9 0.6 copy.9
Async XLA Ops:
  0.0 0.7 copy-start.4
  0.7 1.2 %copy-start = (bf16[1,64,8192]{2,1,0:T(8,128)(2,1)S(1)}, bf16[1,64,8192]{2,1,0:T(8,128)(2,1)}, u32[]{:S(2)}) copy-start(bf16[1,64,8192]{2,1,0:T(8,128)(2,1)} %x_ref.1) | copy-start | bytes 3145732
  1.9 1.2 %copy-start.1 = (bf16[1,512,1024]{2,1,0:T(8,128)(2,1)S(1)}, bf16[1,512,1024]{2,1,0:T(8,128)(2,1)}, u32[]{:S(2)}) copy-start(bf16[1,512,1024]{2,1,0:T(8,128)(2,1)} %k_ref.1) | copy-start | bytes 3145732
  3.1 1.2 %copy-start.2 = (bf16[1,512,1024]{2,1,0:T(8,128)(2,1)S(1)}, bf16[1,512,1024]{2,1,0:T(8,128)(2,1)}, u32[]{:S(2)}) copy-start(bf16[1,512,1024]{2,1,0:T(8,128)(2,1)} %v_ref.1) | copy-start | bytes 3145732
  4.4 0.9 %copy-start.3 = (bf16[512,128]{1,0:T(8,128)(2,1)S(1)}, bf16[512,128]{1,0:T(8,128)(2,1)}, u32[]{:S(2)}) copy-start(bf16[512,128]{1,0:T(8,128)(2,1)} %w_ref.1) | copy-start | bytes 393220

commit v4 on v3

--- a/solution.py
+++ b/solution.py
@@ -178,8 +178,8 @@
     q_slot = unit_of_me * QUAD + quad
 
     def q_copy(i):
-        far = NZ + jnp.where(i % 2 == 1, (i + 1) // 2, -(i // 2))
-        t = lax.rem(z + far, NZ) * QUAD + handler
+        half = NZ // 2
+        t = (half * (i // half) + lax.rem(z + i, half)) * QUAD + handler
         return t, pltpu.make_async_remote_copy(
             src_ref=qown, dst_ref=qbuf.at[unit_of_me, my_rows], send_sem=q_send.at[i], recv_sem=q_recv.at[q_slot],
             device_id=at_seq(t), device_id_type=MESH)

time: 78.8 us -> 78.5 us (level)
  the two profiles are of different devices: /device:TPU:75 before, /device:TPU:73 now
where the time goes in v4:
time: 78.5 us; the launch traced here: 78.2 us
  Pallas kernels  72.3 us (92%)
  local copies, waits for them, and re-layouts  5.18 us (7%)
    pallas_call x1, Pallas kernels, on_device(): pl.pallas_call(kernel, out_shape=jax.ShapeDtypeStruct((1, ROWS, HD), bf),...  72.3 us
    unnamed x11, local copies, waits for them, and re-layouts  5.18 us

profile of v4, /device:TPU:73, one launch (start us, length us, event | category | flops | bytes accessed | tf_op | source)
XLA Modules:
  0.0 78.2 jit_solution(11568698164488958269)
XLA Ops:
  0.0 0.0 copy-start.4
  0.7 0.0 copy-done.4
  0.7 0.0 copy-start
  0.7 1.2 %copy-done = bf16[1,64,8192]{2,1,0:T(8,128)(2,1)S(1)} copy-done((bf16[1,64,8192]{2,1,0:T(8,128)(2,1)S(1)}, bf16[1,64,8192]{2,1,0:T(8,128)(2,1)}, u32[]{:S(2)}) %copy-start) | copy-done | bytes 1048600
  1.9 0.0 copy-start.1
  1.9 1.2 %copy-done.1 = bf16[1,512,1024]{2,1,0:T(8,128)(2,1)S(1)} copy-done((bf16[1,512,1024]{2,1,0:T(8,128)(2,1)S(1)}, bf16[1,512,1024]{2,1,0:T(8,128)(2,1)}, u32[]{:S(2)}) %copy-start.1) | copy-done | bytes 1048600
  3.1 0.0 copy-start.2
  3.1 1.2 %copy-done.2 = bf16[1,512,1024]{2,1,0:T(8,128)(2,1)S(1)} copy-done((bf16[1,512,1024]{2,1,0:T(8,128)(2,1)S(1)}, bf16[1,512,1024]{2,1,0:T(8,128)(2,1)}, u32[]{:S(2)}) %copy-start.2) | copy-done | bytes 1048600
  4.4 0.0 copy-start.3
  4.4 0.9 %copy-done.3 = bf16[512,128]{1,0:T(8,128)(2,1)S(1)} copy-done((bf16[512,128]{1,0:T(8,128)(2,1)S(1)}, bf16[512,128]{1,0:T(8,128)(2,1)}, u32[]{:S(2)}) %copy-start.3) | copy-done | bytes 131096
  5.3 72.3 %shard_map.64 = bf16[1,64,128]{2,1,0:T(8,128)(2,1)S(1)} custom-call(bf16[1,64,8192]{2,1,0:T(8,128)(2,1)S(1)} %copy-done, bf16[512,128]{1,0:T(8,128)(2,1)S(1)} %copy-done.3, bf16[1,512,1024]{2,1,0:T(8,128)(2,1)S(1)} %copy-done.1, bf16[1,512,1024]{2,1,0:T(8,128)(2,1)S(1)} %copy-done.2, s32[1]{0:T(128)S(6)} %copy.8.len_ref, s32[1,64]{1,0:T(1,128)S(1)} %copy-done.4), custom_call_target="tpu_custom_call" | custom-call | tf_op jit(solution)/shard_map/pallas_call | solution.py:328
  77.6 0.6 copy.9
Async XLA Ops:
  0.0 0.7 copy-start.4
  0.7 1.2 %copy-start = (bf16[1,64,8192]{2,1,0:T(8,128)(2,1)S(1)}, bf16[1,64,8192]{2,1,0:T(8,128)(2,1)}, u32[]{:S(2)}) copy-start(bf16[1,64,8192]{2,1,0:T(8,128)(2,1)} %x_ref.1) | copy-start | bytes 3145732
  1.9 1.2 %copy-start.1 = (bf16[1,512,1024]{2,1,0:T(8,128)(2,1)S(1)}, bf16[1,512,1024]{2,1,0:T(8,128)(2,1)}, u32[]{:S(2)}) copy-start(bf16[1,512,1024]{2,1,0:T(8,128)(2,1)} %k_ref.1) | copy-start | bytes 3145732
  3.1 1.2 %copy-start.2 = (bf16[1,512,1024]{2,1,0:T(8,128)(2,1)S(1)}, bf16[1,512,1024]{2,1,0:T(8,128)(2,1)}, u32[]{:S(2)}) copy-start(bf16[1,512,1024]{2,1,0:T(8,128)(2,1)} %v_ref.1) | copy-start | bytes 3145732
  4.4 0.9 %copy-start.3 = (bf16[512,128]{1,0:T(8,128)(2,1)S(1)}, bf16[512,128]{1,0:T(8,128)(2,1)}, u32[]{:S(2)}) copy-start(bf16[512,128]{1,0:T(8,128)(2,1)} %w_ref.1) | copy-start | bytes 393220
